TPU v7x, 32 devices: a whole 2x2x4 slice. The times are simulated.
32 devices in a mesh: copy: 8 (over z, y), head: 4 (over x, core).
Axes of the slice: x: 2, y: 2, z: 4, core: 2. Of those that a mesh axis runs over, the one named last changes fastest.
Arguments:
- query: bfloat16 [8, 16, 48, 512], P('copy', 'head'), may hold values from -6 to 6
- keys: bfloat16 [8, 16, 48, 512], P('copy', 'head'), may hold values from -6 to 6
- values: bfloat16 [8, 16, 48, 512], P('copy', 'head'), may hold values from -6 to 6
- d_gated: bfloat16 [8, 16, 48, 512], P('copy', 'head'), may hold values from -48 to 48
- tokens: bfloat16 [8, 512, 768], P('copy', 'head'), may hold values from -6 to 6
- projections: bfloat16 [4, 16, 48, 768], P(None, 'head'), may hold values from -0.21875 to 0.21875
- pair_bias: bfloat16 [16, 512, 512], P('head'), may hold values from -6 to 6
- pair: bfloat16 [512, 512, 128], P('head', 'copy'), may hold values from -6 to 6
- bias_weight: bfloat16 [128, 16], replicated, may hold values from -1.5 to 1.5
- atom_mask: int32 [512], replicated, may hold values 0 or 1
- token_offsets: int32 [512], replicated, may hold values from 0 to 1536, as said below
Outputs:
- d_tokens: bfloat16 [8, 512, 768], P('copy', 'head')
- d_projections: float32 [4, 16, 48, 768], P(None, 'head')
- d_pair: bfloat16 [512, 512, 128], P('head', 'copy')
- d_bias_weight: float32 [128, 16], replicated
- d_rel_table: float32 [16, 65], replicated
Inputs may be any that keep to these rules, and one draw needn't show every extreme that they name: `token_offsets`: never decreasing along the window, 0 at its first token and 1536 at its last; neighbouring tokens may share a value, and chain breaks leave gaps.
All inputs are finite; a program needn't handle non-finite values.
Results may differ from a plain program's by a relative error of at most 0.025.
Values may be sent and summed in bfloat16 or wider, within the bound.
A program may use at most 64 MiB of HBM per device.

v0:
```python
import math

import jax
import jax.numpy as jnp
from jax import lax
from jax.sharding import PartitionSpec as P

BINS = 65


MASKED_SCORE = -1000000000.0


def shards(
    query,
    keys,
    values,
    d_gated,
    tokens,
    projections,
    pair_bias,
    pair,
    bias_weight,
    atom_mask,
    token_offsets,
):
    score_scale = 1.0 / math.sqrt(query.shape[2])
    gathered = lax.all_gather(tokens, "head", axis=1, tiled=True)
    gate_pre = jnp.einsum(
        "cid,hkd->chki", gathered, projections[3], preferred_element_type=jnp.float32
    )
    gate_open = jax.nn.sigmoid(gate_pre)
    key_valid = (atom_mask > 0)[None, None, None, :]
    block_rows = 512
    scores = (
        jnp.einsum("chkq,chkj->chqj", query, keys, preferred_element_type=jnp.float32) * score_scale
    )
    scores = scores + pair_bias[None, :, 0:block_rows, :].astype(jnp.float32)
    scores = jnp.where(key_valid, scores, MASKED_SCORE)
    row_peak = jnp.max(scores, axis=3, keepdims=True)
    exponent = jnp.exp(scores - row_peak)
    soft_probs = exponent / jnp.sum(exponent, axis=3, keepdims=True)
    weights = soft_probs.astype(jnp.bfloat16)
    attended = jnp.einsum("chqj,chkj->chkq", weights, values, preferred_element_type=jnp.float32)
    upstream = d_gated.astype(jnp.float32)
    d_attended = (upstream * gate_open).astype(jnp.bfloat16)
    gate_parts = (upstream * attended * gate_open * (1.0 - gate_open)).astype(jnp.bfloat16)
    d_probs = jnp.einsum("chkq,chkj->chqj", d_attended, values, preferred_element_type=jnp.float32)
    row_inner = jnp.sum(soft_probs * d_probs, axis=3, keepdims=True)
    d_scores = (soft_probs * (d_probs - row_inner)).astype(jnp.bfloat16)
    value_total = jnp.einsum(
        "chqj,chkq->chkj", weights, d_attended, preferred_element_type=jnp.float32
    )
    query_grad = (
        jnp.einsum("chqj,chkj->chkq", d_scores, keys, preferred_element_type=jnp.float32)
        * score_scale
    )
    query_parts = query_grad.astype(jnp.bfloat16)
    key_total = jnp.einsum("chqj,chkq->chkj", d_scores, query, preferred_element_type=jnp.float32)
    d_keys = (key_total * score_scale).astype(jnp.bfloat16)
    d_values = value_total.astype(jnp.bfloat16)
    cotangents = jnp.stack([query_parts, d_keys, d_values, gate_parts])
    local_sum = jnp.sum(d_scores, axis=0, dtype=jnp.float32).astype(jnp.bfloat16)
    column_sum = lax.psum_scatter(local_sum, "copy", scatter_dimension=2, tiled=True).astype(
        jnp.float32
    )
    d_bias = lax.all_to_all(
        column_sum.astype(jnp.bfloat16), "head", split_axis=1, concat_axis=0, tiled=True
    )
    rows_here = d_bias.shape[1]
    cols_here = d_bias.shape[2]
    d_pair = jnp.einsum(
        "hij,ch->ijc", d_bias, bias_weight, preferred_element_type=jnp.float32
    ).astype(jnp.bfloat16)
    weight_part = jnp.einsum("ijc,hij->ch", pair, d_bias, preferred_element_type=jnp.float32)
    row_anchor = lax.axis_index("head") * rows_here
    col_anchor = lax.axis_index("copy") * cols_here
    row_offsets = lax.dynamic_slice_in_dim(token_offsets, row_anchor, rows_here)
    col_offsets = lax.dynamic_slice_in_dim(token_offsets, col_anchor, cols_here)
    reach_bins = (BINS - 1) // 2
    bin_index = (
        jnp.clip(col_offsets[None, :] - row_offsets[:, None], -reach_bins, reach_bins) + reach_bins
    )
    one_hot = (bin_index[:, :, None] == jnp.arange(BINS, dtype=jnp.int32)[None, None, :]).astype(
        jnp.bfloat16
    )
    table_part = jnp.einsum("hij,ijb->hb", d_bias, one_hot, preferred_element_type=jnp.float32)
    table_sum, weight_sum = lax.psum((table_part, weight_part), ("copy", "head"))
    summed_tokens = lax.psum_scatter(
        jnp.einsum(
            "mchki,mhkd->icd", cotangents, projections, preferred_element_type=jnp.float32
        ).astype(jnp.bfloat16),
        "head",
        scatter_dimension=0,
        tiled=True,
    ).astype(jnp.float32)
    d_tokens = jnp.transpose(summed_tokens, (1, 0, 2)).astype(jnp.bfloat16)
    proj_part = jnp.einsum(
        "mchki,cid->mhkd", cotangents, gathered, preferred_element_type=jnp.float32
    )
    d_projections = lax.psum(proj_part, "copy")
    return (d_tokens, d_projections, d_pair, weight_sum, table_sum)


def solution(mesh):
    in_specs = (
        P("copy", "head", None, None),
        P("copy", "head", None, None),
        P("copy", "head", None, None),
        P("copy", "head", None, None),
        P("copy", "head", None),
        P(None, "head", None, None),
        P("head", None, None),
        P("head", "copy", None),
        P(),
        P(),
        P(),
    )
    out_specs = (
        P("copy", "head", None),
        P(None, "head", None, None),
        P("head", "copy", None),
        P(),
        P(),
    )
    return jax.shard_map(shards, mesh=mesh, in_specs=in_specs, out_specs=out_specs, check_vma=False)
```

profile of v0, /device:TPU:0, one launch (start us, length us, event | category | flops | bytes accessed | tf_op | source)
XLA Modules:
  0.0 254.0 jit_solution(11695860261970745305)
XLA Ops:
  7.2 0.0 copy-start
  7.2 0.0 copy-start.5
  7.2 0.0 copy-start.2
  7.2 0.0 copy-start.3
  7.2 0.0 reduce-scatter.5.cloned.1.call-start
  7.3 10.4 %all_gather.3 = bf16[1,512,768]{2,1,0:T(8,128)(2,1)S(1)} all-gather(bf16[1,128,768]{2,1,0:T(8,128)(2,1)} %param.15), channel_id=1, replica_groups=mesh['copy'=8,'head'=4] {'head'}, dimensions={1}, use_global_device_ids=true | all-gather | bytes 983040 | tf_op jit(solution)/shard_map/all_gather | solution.py:28
  17.6 4.1 %copy.26 = bf16[4,512,512]{1,2,0:T(8,128)(2,1)} copy(bf16[4,512,512]{2,1,0:T(8,128)(2,1)} %param.17) | data formatting | bytes 4194304 | tf_op args[6]
  21.8 0.0 copy-done.5
  21.8 2.2 fusion.13
  24.0 0.0 copy-done.2
  24.0 0.0 copy-done.3
  24.0 5.3 %fusion.75 = (f32[4,512]{1,0:T(4,128)S(1)}, f32[4,512,512]{1,2,0:T(8,128)}) fusion(bf16[4,512,512]{1,2,0:T(8,128)(2,1)} %copy.26, pred[512]{0:T(512)(128)(4,1)S(1)} %broadcast_compare_fusion, bf16[1,4,48,512]{3,2,1,0:T(8,128)(2,1)S(1)} %copy-done.2, bf16[1,4,48,512]{3,2,1,0:T(8,128)(2,1)S(1)} %copy-done.3), kind=kOutput, calls=%fused_computation.67 | convolution fusion | flops 106955264 | bytes 6693376 | tf_op jit(solution)/shard_map/sub | solution.py:41
  29.3 0.0 copy-done.7
  29.3 3.3 %multiply_reduce_fusion = (f32[4,512]{1,0:T(4,128)S(1)}, f32[4,512,512]{1,2,0:T(8,128)S(1)}) fusion(f32[4,512,512]{1,2,0:T(8,128)} %get-tuple-element.18, f32[4,512]{1,0:T(4,128)S(1)} %get-tuple-element.17, bf16[1,4,48,512]{3,2,1,0:T(8,128)(2,1)S(1)} %copy-done.7, f32[4,48,512]{2,1,0:T(8,128)} %fusion.13, bf16[1,4,48,512]{3,2,1,0:T(8,128)(2,1)} %param.14), kind=kOutput, calls=%fused_computation.2 | convolution fusion | flops 104101888 | bytes 9191424 | tf_op jit(solution)/shard_map/chkq,chkj->chqj/dot_general | solution.py:48
  32.6 0.3 copy-done.1
  33.0 2.5 multiply_convert_fusion
  35.5 0.0 reduce-scatter.5.cloned.1.call-update
  35.5 0.0 reduce-scatter.3.cloned.1.call-start
  35.5 4.6 %fusion.20 = bf16[1,1,4,48,512]{4,3,2,1,0:T(8,128)(2,1)} fusion(f32[4,48,512]{2,1,0:T(8,128)} %fusion.13, bf16[1,4,48,512]{3,2,1,0:T(8,128)(2,1)} %param.14, f32[4,512]{1,0:T(4,128)S(1)} %get-tuple-element.17, bf16[4,512,512]{1,2,0:T(8,128)(2,1)} %copy.26, pred[512]{0:T(512)(128)(4,1)S(1)} %broadcast_compare_fusion, ...), kind=kOutput, calls=%fused_computation.33 | convolution fusion | flops 209062400 | bytes 3285504 | tf_op jit(solution)/shard_map/chqj,chkq->chkj/dot_general | solution.py:51
  40.2 4.5 %fusion.23 = bf16[1,1,4,48,512]{4,3,2,1,0:T(8,128)(2,1)} fusion(bf16[1,4,48,512]{3,2,1,0:T(8,128)(2,1)} %param.14, f32[4,48,512]{2,1,0:T(8,128)} %fusion.13, bf16[1,4,48,512]{3,2,1,0:T(8,128)(2,1)S(1)} %copy-done.7, f32[4,512]{1,0:T(4,128)S(1)} %get-tuple-element.17, bf16[4,512,512]{1,2,0:T(8,128)(2,1)} %copy.26, ...), kind=kOutput, calls=%fused_computation.36 | convolution fusion | flops 209259008 | bytes 3482112 | tf_op jit(solution)/shard_map/chqj,chkj->chkq/dot_general | solution.py:44
  44.7 2.1 fusion.21
  46.9 2.3 fusion.22
  49.2 0.0 copy-done.6
  49.2 0.0 copy-done.9
  49.2 0.0 copy-done.10
  49.2 1.7 fusion.8
  50.9 0.0 reduce-scatter.3.cloned.1.call-update
  51.0 0.0 all-reduce.3.cloned.1.call-start
  51.0 3.2 %fusion.30 = f32[4,4,48,768]{3,2,1,0:T(8,128)} fusion(bf16[1,512,768]{2,1,0:T(8,128)(2,1)S(1)} %all_gather.3, bf16[1,1,4,48,512]{4,3,2,1,0:T(8,128)(2,1)} %fusion.23, bf16[1,1,4,48,512]{4,3,2,1,0:T(8,128)(2,1)} %fusion.20, bf16[1,1,4,48,512]{4,3,2,1,0:T(8,128)(2,1)S(1)} %fusion.22, bf16[1,1,4,48,512]{4,3,2,1,0:T(8,128)(2,1)S(1)} %fusion.21), kind=kOutput, calls=%fused_computation.42 | convolution fusion | flops 605159424 | bytes 3932160 | tf_op jit(solution)/shard_map/mchki,cid->mhkd/dot_general | solution.py:98
  54.2 0.0 all-reduce.3.cloned.1.call-update
  54.3 0.0 copy-done.8
  54.3 0.1 dynamic_slice.7
  54.3 0.1 dynamic_slice.6
  54.4 50.1 %reduce-scatter.5.cloned.1.call-done = bf16[4,512,64]{1,2,0:T(8,128)(2,1)} async-done(((bf16[4,512,512]{1,2,0:T(8,128)(2,1)}), bf16[4,512,64]{1,2,0:T(8,128)(2,1)}) %reduce-scatter.5.cloned.1.call-update) | async-done | bytes 262160 | tf_op jit(solution)/shard_map/reduce_scatter | solution.py:64
  104.5 1.3 copy.33
  105.8 1.1 reshape.152
  106.9 3.6 %all-to-all-start = ((bf16[4,2,16384]{2,1,0:T(2,128)(2,1)}), bf16[4,2,16384]{2,1,0:T(2,128)(2,1)S(1)}, u32[]{:S(2)}, u32[]{:S(2)}) async-start(bf16[4,2,16384]{2,1,0:T(2,128)(2,1)} %reshape.152), calls=%async_computation.2 | async-start | bytes 524288 | tf_op jit(solution)/shard_map/all_to_all | solution.py:67
  110.5 0.1 clamp_add_fusion
  110.6 5.7 %all-to-all-done = bf16[4,2,16384]{2,1,0:T(2,128)(2,1)S(1)} async-done(((bf16[4,2,16384]{2,1,0:T(2,128)(2,1)}), bf16[4,2,16384]{2,1,0:T(2,128)(2,1)S(1)}, u32[]{:S(2)}, u32[]{:S(2)}) %all-to-all-start) | async-done | bytes 262176 | tf_op jit(solution)/shard_map/all_to_all | solution.py:67
  116.3 0.3 reshape.153
  116.7 0.3 copy.34
  117.0 0.8 convolution_convert_fusion
  117.8 2.7 %copy.36 = bf16[128,64,128]{2,1,0:T(8,128)(2,1)} copy(bf16[128,64,128]{2,0,1:T(8,128)(2,1)S(1)} %convolution_convert_fusion) | data formatting | bytes 4194304
  120.5 0.5 fusion.24
  120.9 1.2 fusion.25
  122.2 39.8 %all-reduce = (f32[128,16]{0,1:T(8,128)}, f32[16,65]{1,0:T(8,128)}) all-reduce(f32[128,16]{0,1:T(8,128)S(1)} %fusion.25, f32[16,65]{1,0:T(8,128)S(1)} %fusion.24), channel_id=1, replica_groups=mesh['copy'=8,'head'=4] {'copy','head'}, use_global_device_ids=true, to_apply=%region_6.7 | all-reduce | flops 3088 | bytes 24704 | tf_op jit(solution)/shard_map/psum | solution.py:88
  162.0 82.2 %all-reduce.3.cloned.1.call-done = f32[4,4,48,768]{3,2,1,0:T(8,128)} async-done(((f32[4,4,48,768]{3,2,1,0:T(8,128)}), f32[4,4,48,768]{3,2,1,0:T(8,128)}) %all-reduce.3.cloned.1.call-update) | async-done | bytes 2359312 | tf_op jit(solution)/shard_map/psum | solution.py:101
  244.2 3.3 %copy.52 = f32[4,4,48,768]{3,2,1,0:T(8,128)} copy(f32[4,4,48,768]{3,2,1,0:T(8,128)} %all-reduce.3.cloned.1.call-done) | data formatting | bytes 4718592
  (11 shorter events, 0.0 us)
Async XLA Ops:
  7.2 113.8 %copy-start = (bf16[128,64,128]{2,1,0:T(8,128)(2,1)S(1)}, bf16[128,64,128]{2,1,0:T(8,128)(2,1)}, u32[]{:S(2)}) copy-start(bf16[128,64,128]{2,1,0:T(8,128)(2,1)} %param.18) | copy-start | bytes 6291460
  7.2 14.6 %copy-start.5 = (s32[512]{0:T(512)S(1)}, s32[512]{0:T(512)}, u32[]{:S(2)}) copy-start(s32[512]{0:T(512)} %param.20) | copy-start | bytes 6148
  7.2 16.8 %copy-start.2 = (bf16[1,4,48,512]{3,2,1,0:T(8,128)(2,1)S(1)}, bf16[1,4,48,512]{3,2,1,0:T(8,128)(2,1)}, u32[]{:S(2)}) copy-start(bf16[1,4,48,512]{3,2,1,0:T(8,128)(2,1)} %param.12) | copy-start | bytes 589828
  7.2 16.8 %copy-start.3 = (bf16[1,4,48,512]{3,2,1,0:T(8,128)(2,1)S(1)}, bf16[1,4,48,512]{3,2,1,0:T(8,128)(2,1)}, u32[]{:S(2)}) copy-start(bf16[1,4,48,512]{3,2,1,0:T(8,128)(2,1)} %param.11) | copy-start | bytes 589828
  7.2 97.3 %reduce-scatter.5.cloned.1.call-start = ((), (), s32[]{:S(2)}) async-start(), calls=%async_computation.5 | async-start | bytes 2359296 | tf_op jit(solution)/shard_map/reduce_scatter | solution.py:64
  24.0 5.3 %copy-start.7 = (bf16[1,4,48,512]{3,2,1,0:T(8,128)(2,1)S(1)}, bf16[1,4,48,512]{3,2,1,0:T(8,128)(2,1)}, u32[]{:S(2)}) copy-start(bf16[1,4,48,512]{3,2,1,0:T(8,128)(2,1)} %param.13) | copy-start | bytes 589828
  29.3 3.7 %copy-start.1 = (f32[4,512,512]{1,2,0:T(8,128)S(1)}, f32[4,512,512]{1,2,0:T(8,128)}, u32[]{:S(2)}) copy-start(f32[4,512,512]{1,2,0:T(8,128)} %get-tuple-element.18) | copy-start | bytes 12582916
  35.5 126.5 %reduce-scatter.3.cloned.1.call-start = ((), (), s32[]{:S(2)}) async-start(), calls=%async_computation.3 | async-start | bytes 983040 | tf_op jit(solution)/shard_map/reduce_scatter | solution.py:89
  44.7 4.5 %copy-start.6 = (bf16[4,4,48,768]{3,2,1,0:T(8,128)(2,1)S(1)}, bf16[4,4,48,768]{3,2,1,0:T(8,128)(2,1)}, u32[]{:S(2)}) copy-start(bf16[4,4,48,768]{3,2,1,0:T(8,128)(2,1)} %param.16) | copy-start | bytes 3538948
  44.7 4.5 %copy-start.9 = (bf16[1,1,4,48,512]{4,3,2,1,0:T(8,128)(2,1)S(1)}, bf16[1,1,4,48,512]{4,3,2,1,0:T(8,128)(2,1)}, u32[]{:S(2)}) copy-start(bf16[1,1,4,48,512]{4,3,2,1,0:T(8,128)(2,1)} %fusion.20) | copy-start | bytes 589828
  44.7 4.5 %copy-start.10 = (bf16[1,1,4,48,512]{4,3,2,1,0:T(8,128)(2,1)S(1)}, bf16[1,1,4,48,512]{4,3,2,1,0:T(8,128)(2,1)}, u32[]{:S(2)}) copy-start(bf16[1,1,4,48,512]{4,3,2,1,0:T(8,128)(2,1)} %fusion.23) | copy-start | bytes 589828
  50.9 3.3 %copy-start.8 = (s32[512]{0:T(512)S(1)}, s32[512]{0:T(512)}, u32[]{:S(2)}) copy-start(s32[512]{0:T(512)} %param.21) | copy-start | bytes 6148
  51.0 193.3 %all-reduce.3.cloned.1.call-start = ((), (), s32[]{:S(2)}) async-start(), calls=%async_computation.4 | async-start | bytes 4718592 | tf_op jit(solution)/shard_map/psum | solution.py:101
  54.2 62.8 %copy-start.4 = (bf16[128,16]{0,1:T(8,128)(2,1)S(1)}, bf16[128,16]{0,1:T(8,128)(2,1)}, u32[]{:S(2)}) copy-start(bf16[128,16]{0,1:T(8,128)(2,1)} %param.19) | copy-start | bytes 12292
  106.9 9.4 %all-to-all-start = ((bf16[4,2,16384]{2,1,0:T(2,128)(2,1)}), bf16[4,2,16384]{2,1,0:T(2,128)(2,1)S(1)}, u32[]{:S(2)}, u32[]{:S(2)}) async-start(bf16[4,2,16384]{2,1,0:T(2,128)(2,1)} %reshape.152), calls=%async_computation.2 | async-start | bytes 524288 | tf_op jit(solution)/shard_map/all_to_all | solution.py:67
Sparse Core Ops, SparseCore 0:
  35.6 68.8 reduce-scatter.4
  107.6 22.3 reduce-scatter.2
  134.7 109.5 all-reduce.2
where the time goes:
time: 255 us; the launch traced here: 254 us
  waiting for transfers between devices  138 us (54%)
  blocking collectives  50.2 us (20%)
  matrix products  31.8 us (12%)
  between operations  13.9 us (5%)
  local copies, waits for them, and re-layouts  13.7 us (5%)
  starting transfers between devices  3.71 us (1%)
  other arithmetic  2.57 us (1%)
    psum x1, waiting for transfers between devices, shards(): d_projections = lax.psum(proj_part, 'copy')  82.2 us
    reduce_scatter x1, waiting for transfers between devices, shards(): lax.psum_scatter(local_sum, 'copy', scatter_dimension=2, tiled=True)  50.1 us
    psum x1, blocking collectives, shards(): lax.psum((table_part, weight_part), ('copy', 'head'))  39.8 us
    unnamed x27, local copies, waits for them, and re-layouts  11.9 us
    all_gather x1, blocking collectives, shards(): gathered = lax.all_gather(tokens, 'head', axis=1, tiled=True)  10.4 us
    all_to_all x1, waiting for transfers between devices, shards(): lax.all_to_all(column_sum.astype(jnp.bfloat16), 'head', split_axis=1, con...  5.74 us
    sub x1, matrix products, shards(): exponent = jnp.exp(scores - row_peak)  5.32 us
  transfers between devices with their start and end apart: 4, of which 3 were waited for; matrix products, arithmetic and copies ran while one was open for 11% of the time, Pallas kernels for 0%

commit v1 on v0

v1 whole, which is shorter than its diff:
```python
import functools
import math

import jax
import jax.numpy as jnp
from jax import lax
from jax.experimental import pallas as pl
from jax.experimental.pallas import tpu as pltpu
from jax.sharding import PartitionSpec as P

BINS = 65
MASKED_SCORE = -1000000000.0
MESH = pl.DeviceIdType.MESH
F32 = jnp.float32
BF16 = jnp.bfloat16


def contract(a, b, da, db):
    return lax.dot_general(a, b, (((da,), (db,)), ((), ())), preferred_element_type=F32)


def bit_of(index, b):
    return (index // (1 << b)) % 2


def flip(index, b):
    return index + (1 - 2 * bit_of(index, b)) * (1 << b)


def rest(count):
    return (slice(None),) * count


def main_kernel(
    n, nh, scale,
    q_ref, k_ref, v_ref, dg_ref, own_ref, proj_ref, bias_ref, mask_ref,
    dtok_out, dproj_out, dbias_out,
    tok, bt, gate, w_s, ds, cot, dp, pg, dt, sb, rs, ps, ts,
    tok_sem, ds_sem, dp_sem, pg_sem, dt_sem, sb_sem,
):
    lc, lh = n.bit_length() - 1, nh.bit_length() - 1
    heads, hd, t = q_ref.shape
    d = own_ref.shape[1]
    rows = 4 * heads * hd
    tr = t // nh
    j = t // n
    copy = lax.axis_index("copy")
    head = lax.axis_index("head")
    cb = [bit_of(copy, b) for b in range(lc)]
    hb = [bit_of(head, b) for b in range(lh)]

    barrier = pltpu.get_barrier_semaphore()
    for b in range(lc):
        pl.semaphore_signal(barrier, inc=1, device_id={"copy": flip(copy, b)}, device_id_type=MESH)
    for step in range(1, nh):
        pl.semaphore_signal(
            barrier, inc=1, device_id={"head": (head + step) % nh}, device_id_type=MESH
        )
    own_index = tuple(hb[b] for b in reversed(range(lh)))
    tok[own_index] = own_ref[...]
    pl.semaphore_wait(barrier, lc + nh - 1)

    def remote(src, dst, sems, index, device):
        return pltpu.make_async_remote_copy(
            src_ref=src,
            dst_ref=dst,
            send_sem=sems.at[(0,) + index],
            recv_sem=sems.at[(1,) + index],
            device_id=device,
            device_id_type=MESH,
        )

    def spread(ref, bits, b, sems, device):
        at = rest(len(bits) - 1 - b) + tuple(bits[x] for x in reversed(range(b + 1)))
        return remote(ref.at[at], ref.at[at], sems, (b,), device)

    def halve(src, dst, bits, s, sems, index, device, lead=()):
        at = lead + rest(len(bits) - s - 1) + (1 - bits[s],)
        to = dst.at[lead] if lead else dst
        return remote(src.at[at], to, sems, index, device)

    def fold(src, dst, bits, s, lead=()):
        at = lead + rest(len(bits) - s - 1) + (bits[s],)
        whole = lead if lead else Ellipsis
        dst[whole] = (src[at].astype(F32) + dst[whole].astype(F32)).astype(BF16)

    def tok_copy(b):
        return spread(tok, hb, b, tok_sem, {"head": flip(head, b)})

    def ds_copy(h, s):
        src = ds if s == 0 else rs[s - 1]
        return halve(src, rs[s], cb, s, ds_sem, (h, s), {"copy": flip(copy, s)}, (h,))

    def dp_copy(s):
        src = dp if s == 0 else ps[s - 1]
        return halve(src, ps[s], cb, s, dp_sem, (s,), {"copy": flip(copy, s)})

    def pg_copy(b):
        return spread(pg, cb, b, pg_sem, {"copy": flip(copy, b)})

    def dt_copy(s):
        src = dt if s == 0 else ts[s - 1]
        return halve(src, ts[s], hb, s, dt_sem, (s,), {"head": flip(head, s)})

    def sb_copy(step):
        peer = (head + step) % nh
        return remote(sb.at[peer], dbias_out.at[head], sb_sem, (step,), {"head": peer})

    tok_copy(lh - 1).start()

    @pl.loop(0, heads)
    def _(h):
        bt[h] = bias_ref[h].T

    for b in reversed(range(lh)):
        tok_copy(b).wait_recv()
        if b > 0:
            tok_copy(b - 1).start()
    tokens = tok[...].reshape(t, d)
    gate_pre = contract(proj_ref[3 * heads * hd :, :], tokens, 1, 1)
    gate[...] = jax.nn.sigmoid(gate_pre).reshape(heads, hd, t)

    ib = min(t, 256)

    def compute(h):
        valid = mask_ref[...] > 0
        keys, values = k_ref[h], v_ref[h]
        for start in range(0, t, ib):
            cols = pl.ds(start, ib)
            query = q_ref[h, :, cols]
            s = contract(keys, query, 0, 0) * scale + bt[h, :, cols].astype(F32)
            s = jnp.where(valid, s, MASKED_SCORE)
            e = jnp.exp(s - jnp.max(s, axis=0, keepdims=True))
            p = e * (1.0 / jnp.sum(e, axis=0, keepdims=True))
            w = p.astype(BF16)
            w_s[:, cols] = w
            att = contract(values, w, 1, 0)
            g = gate[h, :, cols]
            up = dg_ref[h, :, cols].astype(F32)
            datt = (up * g).astype(BF16)
            cot[2, h, :, cols] = datt
            cot[3, h, :, cols] = (up * att * g * (1.0 - g)).astype(BF16)
            inner = jnp.sum(datt.astype(F32) * att, axis=0, keepdims=True)
            dprob = contract(values, datt, 0, 0)
            dsb = (p * (dprob - inner)).astype(BF16)
            ds[(h,) + rest(lc + 1) + (cols,)] = dsb.reshape((2,) * lc + (j, ib))
            cot[0, h, :, cols] = (contract(keys, dsb, 1, 0) * scale).astype(BF16)

    def finish(h):
        full = ds[h].reshape(t, t)
        cot[1, h] = (contract(q_ref[h], full, 1, 1) * scale).astype(BF16)
        cot[2, h] = contract(cot[2, h], w_s[...], 1, 1).astype(BF16)

    def advance(h, s):
        ds_copy(h, s - 1).wait_recv()
        fold(ds if s == 1 else rs[s - 2], rs[s - 1], cb, s - 1, (h,))
        if s < lc:
            ds_copy(h, s).start()

    @pl.loop(0, heads)
    def _(h):
        compute(h)
        ds_copy(h, 0).start()
        finish(h)
        for s in range(1, lc + 1):

            @pl.when(h >= s)
            def _():
                advance(h - s, s)

    def drain(now):
        for s in range(1, lc + 1):
            if 0 <= now - s < heads:
                advance(now - s, s)

    flat = cot[...].reshape(rows, t)
    part = contract(flat, tok[...].reshape(t, d), 1, 0).astype(BF16)
    sr = dp.shape[-2]
    if rows < n * sr:
        part = jnp.concatenate([part, jnp.zeros((n * sr - rows, d), BF16)], axis=0)
    dp[...] = part.reshape((2,) * lc + (sr, d))
    dp_copy(0).start()
    drain(heads)
    dt[...] = contract(flat, proj_ref[...], 0, 0).astype(BF16).reshape((2,) * lh + (tr, d))
    dt_copy(0).start()
    for now in range(heads + 1, heads + lc):
        drain(now)

    total = rs[lc - 1]
    for peer in range(nh):
        sb[peer] = total[:, :, peer * tr : (peer + 1) * tr]
    for step in range(1, nh):
        sb_copy(step).start()
    dbias_out[head] = sb[head]

    def dp_advance(s):
        dp_copy(s - 1).wait_recv()
        fold(dp if s == 1 else ps[s - 2], ps[s - 1], cb, s - 1)
        if s < lc:
            dp_copy(s).start()

    dp_advance(1)
    for s in range(1, lh + 1):
        dt_copy(s - 1).wait_recv()
        fold(dt if s == 1 else ts[s - 2], ts[s - 1], hb, s - 1)
        if s < lh:
            dt_copy(s).start()
        if s + 1 <= lc:
            dp_advance(s + 1)
    for s in range(lh + 2, lc + 1):
        dp_advance(s)
    dtok_out[...] = ts[lh - 1][...]
    pg[tuple(cb[b] for b in reversed(range(lc)))] = ps[lc - 1][...]
    for b in reversed(range(lc)):
        pg_copy(b).start()
        pg_copy(b).wait_recv()
    dproj_out[...] = pg[...].reshape(n * sr, d)[:rows].astype(F32)
    for step in range(1, nh):
        sb_copy(step).wait()
    for b in range(lh):
        tok_copy(b).wait_send()
        dt_copy(b).wait_send()
    for b in range(lc):
        dp_copy(b).wait_send()
        pg_copy(b).wait_send()

    @pl.loop(0, heads)
    def _(h):
        for s in range(lc):
            ds_copy(h, s).wait_send()


def sum_kernel(n, nh, x_ref, o_ref, first, second, sem_a, sem_b):
    copy = lax.axis_index("copy")
    head = lax.axis_index("head")
    barrier = pltpu.get_barrier_semaphore()
    for step in range(1, n):
        pl.semaphore_signal(
            barrier, inc=1, device_id={"copy": (copy + step) % n}, device_id_type=MESH
        )
    for step in range(1, nh):
        pl.semaphore_signal(
            barrier, inc=1, device_id={"head": (head + step) % nh}, device_id_type=MESH
        )
    first[copy] = x_ref[...]
    pl.semaphore_wait(barrier, n + nh - 2)

    def exchange(buf, me, count, sems, axis):
        def make(step):
            return pltpu.make_async_remote_copy(
                src_ref=buf.at[me],
                dst_ref=buf.at[me],
                send_sem=sems.at[0, step],
                recv_sem=sems.at[1, step],
                device_id={axis: (me + step) % count},
                device_id_type=MESH,
            )

        for step in range(1, count):
            make(step).start()
        for step in range(1, count):
            make(step).wait()
        total = buf[0]
        for index in range(1, count):
            total = total + buf[index]
        return total

    second[head] = exchange(first, copy, n, sem_a, "copy")
    o_ref[...] = exchange(second, head, nh, sem_b, "head")


def vmem():
    return pl.BlockSpec(memory_space=pltpu.VMEM)


def shards(
    n, nh, query, keys, values, d_gated, tokens, projections, pair_bias, pair, bias_weight,
    atom_mask, token_offsets,
):
    heads, hd, t = query.shape[1:]
    d = tokens.shape[2]
    lc, lh = n.bit_length() - 1, nh.bit_length() - 1
    rows = 4 * heads * hd
    tr, j = t // nh, t // n
    sr = -(-rows // (n * 16)) * 16
    args = (
        query[0], keys[0], values[0], d_gated[0], tokens[0], projections.reshape(rows, d),
        pair_bias, atom_mask.reshape(t, 1),
    )
    dma = pltpu.SemaphoreType.DMA
    d_tokens, d_proj, d_bias = pl.pallas_call(
        functools.partial(main_kernel, n, nh, 1.0 / math.sqrt(hd)),
        out_shape=(
            jax.ShapeDtypeStruct((tr, d), BF16),
            jax.ShapeDtypeStruct((rows, d), F32),
            jax.ShapeDtypeStruct((nh, heads, j, tr), BF16),
        ),
        in_specs=[vmem()] * len(args),
        out_specs=(vmem(),) * 3,
        scratch_shapes=[
            pltpu.VMEM((2,) * lh + (tr, d), BF16),
            pltpu.VMEM((heads, t, t), BF16),
            pltpu.VMEM((heads, hd, t), F32),
            pltpu.VMEM((t, t), BF16),
            pltpu.VMEM((heads,) + (2,) * lc + (j, t), BF16),
            pltpu.VMEM((4, heads, hd, t), BF16),
            pltpu.VMEM((2,) * lc + (sr, d), BF16),
            pltpu.VMEM((2,) * lc + (sr, d), BF16),
            pltpu.VMEM((2,) * lh + (tr, d), BF16),
            pltpu.VMEM((nh, heads, j, tr), BF16),
            [pltpu.VMEM((heads,) + (2,) * (lc - s - 1) + (j, t), BF16) for s in range(lc)],
            [pltpu.VMEM((2,) * (lc - s - 1) + (sr, d), BF16) for s in range(lc)],
            [pltpu.VMEM((2,) * (lh - s - 1) + (tr, d), BF16) for s in range(lh)],
            dma((2, lh)), dma((2, heads, lc)), dma((2, lc)), dma((2, lc)), dma((2, lh)),
            dma((2, nh)),
        ],
        compiler_params=pltpu.CompilerParams(
            collective_id=0, has_side_effects=True, vmem_limit_bytes=48 * 2**20
        ),
    )(*args)
    d_bias = d_bias.reshape(nh * heads, j, tr)
    d_pair = jnp.einsum("hji,ch->ijc", d_bias, bias_weight, preferred_element_type=F32).astype(BF16)
    weight_part = jnp.einsum("ijc,hji->hc", pair, d_bias, preferred_element_type=F32)
    row_offsets = lax.dynamic_slice_in_dim(token_offsets, lax.axis_index("head") * tr, tr)
    col_offsets = lax.dynamic_slice_in_dim(token_offsets, lax.axis_index("copy") * j, j)
    reach = (BINS - 1) // 2
    bin_index = jnp.clip(col_offsets[:, None] - row_offsets[None, :], -reach, reach) + reach
    one_hot = (bin_index[:, :, None] == jnp.arange(BINS, dtype=jnp.int32)[None, None, :]).astype(
        BF16
    )
    table_part = jnp.einsum("hji,jib->hb", d_bias, one_hot, preferred_element_type=F32)
    wide = -(-BINS // 128) * 128
    both = jnp.concatenate([weight_part, jnp.pad(table_part, ((0, 0), (0, wide - BINS)))], axis=1)
    summed = pl.pallas_call(
        functools.partial(sum_kernel, n, nh),
        out_shape=jax.ShapeDtypeStruct(both.shape, F32),
        in_specs=[vmem()],
        out_specs=vmem(),
        scratch_shapes=[
            pltpu.VMEM((n,) + both.shape, F32),
            pltpu.VMEM((nh,) + both.shape, F32),
            dma((2, n)),
            dma((2, nh)),
        ],
        compiler_params=pltpu.CompilerParams(collective_id=1, has_side_effects=True),
    )(both)
    channels = bias_weight.shape[0]
    return (
        d_tokens[None],
        d_proj.reshape(projections.shape),
        d_pair,
        summed[:, :channels].T,
        summed[:, channels : channels + BINS],
    )


def solution(mesh):
    in_specs = (
        P("copy", "head", None, None),
        P("copy", "head", None, None),
        P("copy", "head", None, None),
        P("copy", "head", None, None),
        P("copy", "head", None),
        P(None, "head", None, None),
        P("head", None, None),
        P("head", "copy", None),
        P(),
        P(),
        P(),
    )
    out_specs = (
        P("copy", "head", None),
        P(None, "head", None, None),
        P("head", "copy", None),
        P(),
        P(),
    )
    body = functools.partial(shards, mesh.shape["copy"], mesh.shape["head"])
    return jax.shard_map(body, mesh=mesh, in_specs=in_specs, out_specs=out_specs, check_vma=False)
```

time: 255 us -> 130 us (0.51)
  waiting for transfers between devices: 138 us -> 0 us
  Pallas kernels: 0 us -> 108 us
  blocking collectives: 50.2 us -> 0 us
  matrix products: 31.8 us -> 1.75 us
  between operations: 13.9 us -> 0.74 us
  local copies, waits for them, and re-layouts: 13.7 us -> 17.8 us
  starting transfers between devices: 3.71 us -> 0 us
    pallas_call x0 -> x2, Pallas kernels: none -> 108 us  [the longest x1 94.9 us: shards(): pl.pallas_call(functools.partial(main_kernel, n, nh, 1.0 / math.sqrt(hd))...]
    psum x1 -> x0, waiting for transfers between devices: 82.2 us -> none  [shards(): d_projections = lax.psum(proj_part, 'copy')]
    reduce_scatter x2 -> x0, waiting for transfers between devices: 50.1 us -> none  [the longest x1 50.1 us: shards(): lax.psum_scatter(local_sum, 'copy', scatter_dimension=2, tiled=True)]
    psum x1 -> x0, blocking collectives: 39.8 us -> none  [shards(): lax.psum((table_part, weight_part), ('copy', 'head'))]
    dot_general x11 -> x3, matrix products: 26.5 us -> 1.75 us  [the longest x1 0.77 us: shards(): jnp.einsum('hji,ch->ijc', d_bias, bias_weight, preferred_element_type=F32)]
    all_gather x1 -> x0, blocking collectives: 10.4 us -> none  [shards(): gathered = lax.all_gather(tokens, 'head', axis=1, tiled=True)]
    all_to_all x1 -> x0, waiting for transfers between devices: 5.74 us -> none  [shards(): lax.all_to_all(column_sum.astype(jnp.bfloat16), 'head', split_axis=1, con...]
    sub x1 -> x0, matrix products: 5.32 us -> none  [shards(): exponent = jnp.exp(scores - row_peak)]
  transfers between devices with their start and end apart: 4 -> 0, of which waited for: 3 -> 0; matrix products, arithmetic and copies ran while one was open for 11% -> 0% of each run, Pallas kernels for 0% -> 0%
where the time goes in v1:
time: 130 us; the launch traced here: 129 us
  Pallas kernels  108 us (83%)
  local copies, waits for them, and re-layouts  17.8 us (14%)
  matrix products  1.75 us (1%)
    pallas_call x1, Pallas kernels, shards(): pl.pallas_call(functools.partial(main_kernel, n, nh, 1.0 / math.sqrt(hd))...  94.9 us
    pallas_call x1, Pallas kernels, shards(): pl.pallas_call(functools.partial(sum_kernel, n, nh), out_shape=jax.ShapeD...  13.5 us
    unnamed x23, local copies, waits for them, and re-layouts  12.3 us

profile of v1, /device:TPU:0, one launch (start us, length us, event | category | flops | bytes accessed | tf_op | source)
XLA Modules:
  0.0 129.4 jit_solution(8658979414235597030)
XLA Ops:
  0.6 0.0 copy-start
  0.7 0.9 dynamic_slice.7
  1.6 0.8 dynamic_slice.6
  2.3 0.1 clamp_add_fusion
  2.4 0.8 copy.21.mask_ref
  3.2 0.0 copy-start.1
  3.2 1.6 %copy-done.1 = bf16[4,512,512]{2,1,0:T(8,128)(2,1)S(1)} copy-done((bf16[4,512,512]{2,1,0:T(8,128)(2,1)S(1)}, bf16[4,512,512]{2,1,0:T(8,128)(2,1)}, u32[]{:S(2)}) %copy-start.1) | copy-done | bytes 2097176
  4.8 0.0 copy-start.2
  4.8 1.3 copy-done.2
  6.1 0.0 copy-start.3
  6.1 0.9 copy-done.3
  7.0 0.0 copy-start.4
  7.0 0.9 copy-done.4
  7.9 0.0 copy-start.5
  8.0 0.9 copy-done.5
  8.9 0.0 copy-start.6
  8.9 0.9 copy-done.6
  9.8 0.0 copy-start.7
  9.8 0.9 copy-done.7
  10.7 94.9 %shard_map.146 = (bf16[128,768]{1,0:T(8,128)(2,1)S(1)}, f32[768,768]{1,0:T(8,128)}, bf16[4,4,64,128]{3,2,1,0:T(8,128)(2,1)S(1)}) custom-call(bf16[4,48,512]{2,1,0:T(8,128)(2,1)S(1)} %bitcast.27, bf16[4,48,512]{2,1,0:T(8,128)(2,1)S(1)} %bitcast.28, bf16[4,48,512]{2,1,0:T(8,128)(2,1)S(1)} %bitcast.29, bf16[4,48,512]{2,1,0:T(8,128)(2,1)S(1)} %bitcast.30, ...), custom_call_target="tpu_custom_call" | custom-call | tf_op jit(solution)/shard_map/pallas_call | solution.py:291
  105.6 0.0 copy-start.9
  105.7 0.5 fusion.2
  106.2 0.4 copy.27
  106.6 0.0 copy-done
  106.7 0.4 convolution_bitcast_fusion
  107.1 0.6 select_maximum_fusion.x_ref
  107.7 13.5 %shard_map.147 = f32[16,256]{1,0:T(8,128)} custom-call(f32[16,256]{1,0:T(8,128)} %select_maximum_fusion.x_ref), custom_call_target="tpu_custom_call" | custom-call | tf_op jit(solution)/shard_map/pallas_call | solution.py:334
  121.3 1.3 %slice.7 = f32[16,65]{1,0:T(8,128)} slice(f32[16,256]{1,0:T(8,128)} %shard_map.147), slice={[0:16], [128:193]} | slice | bytes 8320 | tf_op jit(solution)/shard_map/slice | solution.py:353
  122.6 1.3 %slice_bitcast_fusion = f32[128,16]{0,1:T(8,128)} fusion(f32[16,256]{1,0:T(8,128)} %shard_map.147), kind=kLoop, calls=%fused_computation.11 | loop fusion | bytes 16384 | tf_op jit(solution)/shard_map/transpose | solution.py:352
  123.9 0.0 copy-done.9
  123.9 0.8 convert_bitcast_fusion
  124.6 0.0 copy-start.8
  124.7 2.7 %copy.26 = bf16[128,64,128]{2,1,0:T(8,128)(2,1)} copy(bf16[128,64,128]{2,0,1:T(8,128)(2,1)S(1)} %convert_bitcast_fusion) | data formatting | bytes 4194304
  127.3 0.7 copy.36
  128.0 0.0 copy-done.8
  128.0 1.4 %copy.37 = f32[4,4,48,768]{3,2,1,0:T(8,128)} copy(f32[4,4,48,768]{3,2,1,0:T(8,128)S(1)} %bitcast.33) | data formatting | bytes 4718592
Async XLA Ops:
  0.6 106.0 %copy-start = (bf16[128,64,128]{2,1,0:T(8,128)(2,1)S(1)}, bf16[128,64,128]{2,1,0:T(8,128)(2,1)}, u32[]{:S(2)}) copy-start(bf16[128,64,128]{2,1,0:T(8,128)(2,1)} %param.18) | copy-start | bytes 6291460
  3.2 1.6 %copy-start.1 = (bf16[4,512,512]{2,1,0:T(8,128)(2,1)S(1)}, bf16[4,512,512]{2,1,0:T(8,128)(2,1)}, u32[]{:S(2)}) copy-start(bf16[4,512,512]{2,1,0:T(8,128)(2,1)} %bias_ref.1) | copy-start | bytes 6291460
  4.8 1.3 copy-start.2
  6.1 0.9 copy-start.3
  7.0 0.9 copy-start.4
  7.9 0.9 copy-start.5
  8.9 0.9 copy-start.6
  9.8 0.9 copy-start.7
  105.6 18.2 %copy-start.9 = (bf16[128,16]{0,1:T(8,128)(2,1)S(1)}, bf16[128,16]{0,1:T(8,128)(2,1)}, u32[]{:S(2)}) copy-start(bf16[128,16]{0,1:T(8,128)(2,1)} %param.19) | copy-start | bytes 12292
  124.6 3.4 %copy-start.8 = (f32[768,768]{1,0:T(8,128)S(1)}, f32[768,768]{1,0:T(8,128)}, u32[]{:S(2)}) copy-start(f32[768,768]{1,0:T(8,128)} %get-tuple-element.9) | copy-start | bytes 7077892

commit v2 on v1

v2 whole, which is shorter than its diff:
```python
import functools
import math

import jax
import jax.numpy as jnp
from jax import lax
from jax.experimental import pallas as pl
from jax.experimental.pallas import tpu as pltpu
from jax.sharding import PartitionSpec as P

BINS = 65
MASKED_SCORE = -1000000000.0
MESH = pl.DeviceIdType.MESH
F32 = jnp.float32
BF16 = jnp.bfloat16


def contract(a, b, da, db):
    return lax.dot_general(a, b, (((da,), (db,)), ((), ())), preferred_element_type=F32)


def bit_of(index, b):
    return (index // (1 << b)) % 2


def flip(index, b):
    return index + (1 - 2 * bit_of(index, b)) * (1 << b)


def rest(count):
    return (slice(None),) * count


def main_kernel(
    n, nh, scale,
    off_ref, q_hbm, k_hbm, v_hbm, dg_hbm, own_hbm, proj_hbm, bias_hbm, pair_hbm, bw_ref, mask_ref,
    offrow_ref,
    dtok_out, dproj_out, dpair_out, sums_out,
    q_ref, k_ref, v_ref, dg_ref, proj_ref, bias_ref, pair_ref,
    valid_s, off_s, tok, bt, gate, w_s, ds, cot, dt, sb, rb, xs, first, second, dp, pg, rs, ps, ts,
    in_sem, tok_sem, ds_sem, dp_sem, pg_sem, dt_sem, sb_sem, first_sem, second_sem,
):
    lc, lh = n.bit_length() - 1, nh.bit_length() - 1
    heads, hd, t = q_ref.shape
    d = own_hbm.shape[1]
    rows = 4 * heads * hd
    tr = t // nh
    j = t // n
    halves = len(dp)
    dh = d // halves
    copy = lax.axis_index("copy")
    head = lax.axis_index("head")
    cb = [bit_of(copy, b) for b in range(lc)]
    hb = [bit_of(head, b) for b in range(lh)]
    up_order = tuple(range(lc))
    orders = (up_order[1:] + up_order[:1], up_order)

    barrier = pltpu.get_barrier_semaphore()
    for step in range(1, n):
        pl.semaphore_signal(
            barrier, inc=1, device_id={"copy": (copy + step) % n}, device_id_type=MESH
        )
    for step in range(1, nh):
        pl.semaphore_signal(
            barrier, inc=1, device_id={"head": (head + step) % nh}, device_id_type=MESH
        )
    own_index = tuple(hb[b] for b in reversed(range(lh)))
    loads = [
        pltpu.make_async_copy(src, dst, in_sem.at[index])
        for index, (src, dst) in enumerate((
            (own_hbm, tok.at[own_index]), (bias_hbm, bias_ref), (proj_hbm, proj_ref),
            (q_hbm, q_ref), (k_hbm, k_ref), (v_hbm, v_ref), (dg_hbm, dg_ref),
            (pair_hbm, pair_ref),
        ))
    ]
    for load in loads:
        load.start()

    def remote(src, dst, sems, index, device):
        return pltpu.make_async_remote_copy(
            src_ref=src,
            dst_ref=dst,
            send_sem=sems.at[(0,) + index],
            recv_sem=sems.at[(1,) + index],
            device_id=device,
            device_id_type=MESH,
        )

    def pick(order, bits, s, other):
        left = sorted(order[s:], reverse=True)
        bit = bits[order[s]]
        return rest(left.index(order[s])) + ((1 - bit if other else bit),)

    def halve(src, dst, order, bits, s, sems, index, device, lead=()):
        to = dst.at[lead] if lead else dst
        return remote(src.at[lead + pick(order, bits, s, True)], to, sems, index, device)

    def fold(src, dst, order, bits, s, lead=()):
        whole = lead if lead else Ellipsis
        mine = src[lead + pick(order, bits, s, False)]
        dst[whole] = (mine.astype(F32) + dst[whole].astype(F32)).astype(BF16)

    def spread(ref, order, bits, s, sems, index, device):
        done = order[s + 1 :]
        at = tuple(
            slice(None) if b in done else bits[b] for b in reversed(range(len(bits)))
        )
        return remote(ref.at[at], ref.at[at], sems, index, device)

    def tok_copy(b):
        return spread(tok, tuple(range(lh)), hb, b, tok_sem, (b,), {"head": flip(head, b)})

    def ds_copy(h, s):
        src = ds if s == 0 else rs[s - 1]
        return halve(
            src, rs[s], up_order, cb, s, ds_sem, (h, s), {"copy": flip(copy, s)}, (h,)
        )

    def dp_copy(c, s):
        src = dp[c] if s == 0 else ps[c][s - 1]
        device = {"copy": flip(copy, orders[c][s])}
        return halve(src, ps[c][s], orders[c], cb, s, dp_sem, (c, s), device)

    def pg_copy(c, s):
        device = {"copy": flip(copy, orders[c][s])}
        return spread(pg[c], orders[c], cb, s, pg_sem, (c, s), device)

    def dt_copy(s):
        src = dt if s == 0 else ts[s - 1]
        return halve(
            src, ts[s], tuple(range(lh)), hb, s, dt_sem, (s,), {"head": flip(head, s)}
        )

    def sb_copy(step):
        peer = (head + step) % nh
        return remote(sb.at[peer], rb.at[head], sb_sem, (step,), {"head": peer})

    def first_copy(step):
        here = first.at[copy]
        return remote(here, here, first_sem, (step,), {"copy": (copy + step) % n})

    def second_copy(step):
        here = second.at[head]
        return remote(here, here, second_sem, (step,), {"head": (head + step) % nh})

    loads[0].wait()
    pl.semaphore_wait(barrier, n + nh - 2)
    tok_copy(lh - 1).start()
    wide = valid_s.shape[1]
    valid_s[...] = jnp.broadcast_to(mask_ref[...].astype(F32), (wide, t)).T
    off_s[...] = jnp.broadcast_to(offrow_ref[...].astype(F32), (wide, t)).T
    loads[1].wait()

    @pl.loop(0, heads)
    def _(h):
        bt[h] = bias_ref[h].T

    for b in reversed(range(lh)):
        tok_copy(b).wait_recv()
        if b > 0:
            tok_copy(b - 1).start()
    for load in loads[2:]:
        load.wait()
    tokens = tok[...].reshape(t, d)
    gate_pre = contract(proj_ref[3 * heads * hd :, :], tokens, 1, 1)
    gate[...] = jax.nn.sigmoid(gate_pre).reshape(heads, hd, t)

    ib = min(t, 256)

    def compute(h):
        valid = valid_s[:, 0:1] > 0.5
        keys, values = k_ref[h], v_ref[h]
        for start in range(0, t, ib):
            cols = pl.ds(start, ib)
            query = q_ref[h, :, cols]
            s = contract(keys, query, 0, 0) * scale + bt[h, :, cols].astype(F32)
            s = jnp.where(valid, s, MASKED_SCORE)
            e = jnp.exp(s - jnp.max(s, axis=0, keepdims=True))
            p = e * (1.0 / jnp.sum(e, axis=0, keepdims=True))
            w = p.astype(BF16)
            w_s[:, cols] = w
            att = contract(values, w, 1, 0)
            g = gate[h, :, cols]
            up = dg_ref[h, :, cols].astype(F32)
            datt = (up * g).astype(BF16)
            cot[2, h, :, cols] = datt
            cot[3, h, :, cols] = (up * att * g * (1.0 - g)).astype(BF16)
            inner = jnp.sum(datt.astype(F32) * att, axis=0, keepdims=True)
            dprob = contract(values, datt, 0, 0)
            dsb = (p * (dprob - inner)).astype(BF16)
            ds[(h,) + rest(lc + 1) + (cols,)] = dsb.reshape((2,) * lc + (j, ib))
            cot[0, h, :, cols] = (contract(keys, dsb, 1, 0) * scale).astype(BF16)

    def finish(h):
        full = ds[h].reshape(t, t)
        cot[1, h] = (contract(q_ref[h], full, 1, 1) * scale).astype(BF16)
        cot[2, h] = contract(cot[2, h], w_s[...], 1, 1).astype(BF16)

    def advance(h, s):
        ds_copy(h, s - 1).wait_recv()
        fold(ds if s == 1 else rs[s - 2], rs[s - 1], up_order, cb, s - 1, (h,))
        if s < lc:
            ds_copy(h, s).start()

    @pl.loop(0, heads)
    def _(h):
        compute(h)
        ds_copy(h, 0).start()
        finish(h)
        for s in range(1, lc + 1):

            @pl.when(h >= s)
            def _():
                advance(h - s, s)

    def drain(now):
        for s in range(1, lc + 1):
            if 0 <= now - s < heads:
                advance(now - s, s)

    def dp_advance(c, s):
        dp_copy(c, s - 1).wait_recv()
        fold(dp[c] if s == 1 else ps[c][s - 2], ps[c][s - 1], orders[c], cb, s - 1)
        if s < lc:
            dp_copy(c, s).start()

    def dt_advance(s):
        dt_copy(s - 1).wait_recv()
        fold(dt if s == 1 else ts[s - 2], ts[s - 1], tuple(range(lh)), hb, s - 1)
        if s < lh:
            dt_copy(s).start()

    flat = cot[...].reshape(rows, t)
    sr = dp[0].shape[-2]
    for c in range(halves):
        tokens = tok[...].reshape(t, d)[:, c * dh : (c + 1) * dh]
        part = contract(flat, tokens, 1, 0).astype(BF16)
        if rows < n * sr:
            part = jnp.concatenate([part, jnp.zeros((n * sr - rows, dh), BF16)], axis=0)
        dp[c][...] = part.reshape((2,) * lc + (sr, dh))
        dp_copy(c, 0).start()
    drain(heads)
    dt[...] = contract(flat, proj_ref[...], 0, 0).astype(BF16).reshape((2,) * lh + (tr, d))
    dt_copy(0).start()
    drain(heads + 1)
    dp_advance(0, 1)
    for now in range(heads + 2, heads + lc):
        drain(now)

    total = rs[lc - 1]
    for peer in range(nh):
        sb[peer] = total[:, :, peer * tr : (peer + 1) * tr]
    for step in range(1, nh):
        sb_copy(step).start()
    rb[head] = sb[head]

    for s in range(1, lc):
        if s <= lh:
            dt_advance(s)
        dp_advance(1, s)
        dp_advance(0, s + 1)
    for s in range(lc, lh + 1):
        dt_advance(s)
    dtok_out[...] = ts[lh - 1][...]
    mine = tuple(cb[b] for b in reversed(range(lc)))
    pg[0][mine] = ps[0][lc - 1][...]
    pg_copy(0, lc - 1).start()
    dp_advance(1, lc)
    pg[1][mine] = ps[1][lc - 1][...]
    pg_copy(1, lc - 1).start()

    def pg_advance(s):
        for c in range(halves):
            pg_copy(c, s).wait_recv()
            if s > 0:
                pg_copy(c, s - 1).start()

    for step in range(1, nh):
        sb_copy(step).wait()
    for peer in range(nh):
        for h in range(heads):
            xs[:, peer * heads + h, :] = rb[peer, h].astype(F32).T
    columns = off_s[pl.ds(pl.multiple_of(copy * j, j), j), :]
    bins = lax.broadcasted_iota(jnp.int32, (j, wide), 1).astype(F32)
    reach = (BINS - 1) // 2
    group = 8
    channels = bw_ref.shape[0]

    def pairs(g, acc):
        for u in range(group):
            i = g * group + u
            x = xs[i].astype(BF16)
            dpair_out[i] = contract(x, bw_ref[...], 0, 1).astype(BF16)
            gap = columns - off_ref[head * tr + i].astype(F32)
            hot = jnp.clip(gap, -reach, reach) + reach == bins
            right = jnp.concatenate([pair_ref[i], hot.astype(F32).astype(BF16)], axis=1)
            acc = acc + contract(x, right, 1, 0)
        return acc

    acc = jnp.zeros((nh * heads, channels + wide), F32)
    acc = lax.fori_loop(0, tr // group // 2, pairs, acc)
    pg_advance(lc - 1)
    acc = lax.fori_loop(tr // group // 2, tr // group, pairs, acc)
    first[copy] = acc
    for step in range(1, n):
        first_copy(step).start()
    for s in reversed(range(1, lc - 1)):
        pg_advance(s)
    for step in range(1, n):
        first_copy(step).wait()
    acc = first[0]
    for index in range(1, n):
        acc = acc + first[index]
    second[head] = acc
    for step in range(1, nh):
        second_copy(step).start()
    pg_advance(0)
    for c in range(halves):
        dproj_out[:, c * dh : (c + 1) * dh] = pg[c][...].reshape(n * sr, dh)[:rows]
    for step in range(1, nh):
        second_copy(step).wait()
    acc = second[0]
    for index in range(1, nh):
        acc = acc + second[index]
    sums_out[...] = acc
    for b in range(lh):
        tok_copy(b).wait_send()
        dt_copy(b).wait_send()
    for c in range(halves):
        for b in range(lc):
            dp_copy(c, b).wait_send()
            pg_copy(c, b).wait_send()

    @pl.loop(0, heads)
    def _(h):
        for s in range(lc):
            ds_copy(h, s).wait_send()


def shards(
    n, nh, query, keys, values, d_gated, tokens, projections, pair_bias, pair, bias_weight,
    atom_mask, token_offsets,
):
    heads, hd, t = query.shape[1:]
    d = tokens.shape[2]
    lc, lh = n.bit_length() - 1, nh.bit_length() - 1
    rows = 4 * heads * hd
    tr, j = t // nh, t // n
    sr = -(-rows // (n * 16)) * 16
    channels = bias_weight.shape[0]
    wide = -(-BINS // 128) * 128
    halves = 2
    dh = d // halves
    args = (
        token_offsets, query[0], keys[0], values[0], d_gated[0], tokens[0],
        projections.reshape(rows, d), pair_bias, pair, bias_weight, atom_mask.reshape(1, t),
        token_offsets.reshape(1, t),
    )

    def vmem():
        return pl.BlockSpec(memory_space=pltpu.VMEM)

    hbm = pl.BlockSpec(memory_space=pltpu.HBM)
    dma = pltpu.SemaphoreType.DMA
    heads_all = nh * heads
    sums = (heads_all, channels + wide)
    d_tokens, d_proj, d_pair, summed = pl.pallas_call(
        functools.partial(main_kernel, n, nh, 1.0 / math.sqrt(hd)),
        out_shape=(
            jax.ShapeDtypeStruct((tr, d), BF16),
            jax.ShapeDtypeStruct((rows, d), BF16),
            jax.ShapeDtypeStruct((tr, j, channels), BF16),
            jax.ShapeDtypeStruct(sums, F32),
        ),
        in_specs=[pl.BlockSpec(memory_space=pltpu.SMEM)] + [hbm] * 8 + [vmem()] * 3,
        out_specs=(vmem(),) * 4,
        scratch_shapes=[
            pltpu.VMEM((heads, hd, t), BF16),
            pltpu.VMEM((heads, hd, t), BF16),
            pltpu.VMEM((heads, hd, t), BF16),
            pltpu.VMEM((heads, hd, t), BF16),
            pltpu.VMEM((rows, d), BF16),
            pltpu.VMEM((heads, t, t), BF16),
            pltpu.VMEM((tr, j, channels), BF16),
            pltpu.VMEM((t, wide), F32),
            pltpu.VMEM((t, wide), F32),
            pltpu.VMEM((2,) * lh + (tr, d), BF16),
            pltpu.VMEM((heads, t, t), BF16),
            pltpu.VMEM((heads, hd, t), F32),
            pltpu.VMEM((t, t), BF16),
            pltpu.VMEM((heads,) + (2,) * lc + (j, t), BF16),
            pltpu.VMEM((4, heads, hd, t), BF16),
            pltpu.VMEM((2,) * lh + (tr, d), BF16),
            pltpu.VMEM((nh, heads, j, tr), BF16),
            pltpu.VMEM((nh, heads, j, tr), BF16),
            pltpu.VMEM((tr, heads_all, j), F32),
            pltpu.VMEM((n,) + sums, F32),
            pltpu.VMEM((nh,) + sums, F32),
            [pltpu.VMEM((2,) * lc + (sr, dh), BF16) for c in range(halves)],
            [pltpu.VMEM((2,) * lc + (sr, dh), BF16) for c in range(halves)],
            [pltpu.VMEM((heads,) + (2,) * (lc - s - 1) + (j, t), BF16) for s in range(lc)],
            [
                [pltpu.VMEM((2,) * (lc - s - 1) + (sr, dh), BF16) for s in range(lc)]
                for c in range(halves)
            ],
            [pltpu.VMEM((2,) * (lh - s - 1) + (tr, d), BF16) for s in range(lh)],
            dma((8,)), dma((2, lh)), dma((2, heads, lc)), dma((2, halves, lc)),
            dma((2, halves, lc)), dma((2, lh)), dma((2, nh)), dma((2, n)), dma((2, nh)),
        ],
        compiler_params=pltpu.CompilerParams(
            collective_id=0, has_side_effects=True, vmem_limit_bytes=50 * 2**20
        ),
    )(*args)
    return (
        d_tokens[None],
        d_proj.astype(F32).reshape(projections.shape),
        d_pair,
        summed[:, :channels].T,
        summed[:, channels : channels + BINS],
    )


def solution(mesh):
    in_specs = (
        P("copy", "head", None, None),
        P("copy", "head", None, None),
        P("copy", "head", None, None),
        P("copy", "head", None, None),
        P("copy", "head", None),
        P(None, "head", None, None),
        P("head", None, None),
        P("head", "copy", None),
        P(),
        P(),
        P(),
    )
    out_specs = (
        P("copy", "head", None),
        P(None, "head", None, None),
        P("head", "copy", None),
        P(),
        P(),
    )
    body = functools.partial(shards, mesh.shape["copy"], mesh.shape["head"])
    return jax.shard_map(body, mesh=mesh, in_specs=in_specs, out_specs=out_specs, check_vma=False)
```

time: 130 us -> 104 us (0.80)
  Pallas kernels: 108 us -> 89.8 us
  local copies, waits for them, and re-layouts: 17.8 us -> 11.3 us
  matrix products: 1.75 us -> 0 us
    pallas_call x1 -> x0, Pallas kernels: 13.5 us -> none  [shards(): pl.pallas_call(functools.partial(sum_kernel, n, nh), out_shape=jax.ShapeD...]
    pallas_call x1, Pallas kernels: 94.9 us -> 89.8 us  [shards(): pl.pallas_call(functools.partial(main_kernel, n, nh, 1.0 / math.sqrt(hd))...]
    unnamed x23 -> x21, local copies, waits for them, and re-layouts: 12.3 us -> 10.1 us
    dot_general x3 -> x0, matrix products: 1.75 us -> none  [the longest x1 0.77 us: shards(): jnp.einsum('hji,ch->ijc', d_bias, bias_weight, preferred_element_type=F32)]
    dynamic_slice x2 -> x0, local copies, waits for them, and re-layouts: 1.66 us -> none  [the longest x1 0.9 us: shards(): lax.dynamic_slice_in_dim(token_offsets, lax.axis_index('head') * tr, tr)]
    reshape x0 -> x1, other arithmetic: none -> 1.65 us  [shards(): d_proj.astype(F32).reshape(projections.shape)]
where the time goes in v2:
time: 104 us; the launch traced here: 103 us
  Pallas kernels  89.8 us (86%)
  local copies, waits for them, and re-layouts  11.3 us (11%)
  other arithmetic  1.65 us (2%)
    pallas_call x1, Pallas kernels, shards(): pl.pallas_call(functools.partial(main_kernel, n, nh, 1.0 / math.sqrt(hd))...  89.8 us
    unnamed x21, local copies, waits for them, and re-layouts  10.1 us

profile of v2, /device:TPU:0, one launch (start us, length us, event | category | flops | bytes accessed | tf_op | source)
XLA Modules:
  0.0 103.3 jit_solution(7908449494605931433)
XLA Ops:
  0.6 0.8 copy.16.bw_ref
  1.4 0.0 copy-start
  1.4 1.3 %copy-done = bf16[4,4,48,768]{3,2,1,0:T(8,128)(2,1)S(1)} copy-done((bf16[4,4,48,768]{3,2,1,0:T(8,128)(2,1)S(1)}, bf16[4,4,48,768]{3,2,1,0:T(8,128)(2,1)}, u32[]{:S(2)}) %copy-start) | copy-done | bytes 1179672
  2.7 0.0 copy-start.1
  2.7 0.9 copy-done.1
  3.6 0.0 copy-start.2
  3.6 0.9 copy-done.2
  4.6 0.0 copy-start.3
  4.6 0.9 copy-done.3
  5.5 0.0 copy-start.4
  5.5 0.9 copy-done.4
  6.4 0.0 copy-start.5
  6.4 0.9 copy-done.5
  7.3 0.0 copy-start.6
  7.3 0.7 copy-done.6
  8.0 0.0 copy-start.7
  8.0 0.7 copy-done.7
  8.7 89.8 %shard_map.146 = (bf16[128,768]{1,0:T(8,128)(2,1)S(1)}, bf16[768,768]{1,0:T(8,128)(2,1)S(1)}, bf16[128,64,128]{2,1,0:T(8,128)(2,1)}, f32[16,256]{1,0:T(8,128)S(1)}) custom-call(s32[512]{0:T(512)S(1)} %copy-done.6, bf16[4,48,512]{2,1,0:T(8,128)(2,1)S(1)} %bitcast.15, bf16[4,48,512]{2,1,0:T(8,128)(2,1)S(1)} %bitcast.16, bf16[4,48,512]{2,1,0:T(8,128)(2,1)S(1)} %bitcast.17, ...), custom_call_target="tpu_custom_call" | custom-call | tf_op jit(solution)/shard_map/pallas_call | solution.py:367
  98.5 0.0 copy-start.8
  98.5 0.6 slice.7
  99.1 0.6 slice_bitcast_fusion
  99.7 1.6 %convert.1 = f32[4,4,48,768]{3,2,1,0:T(8,128)} convert(bf16[4,4,48,768]{3,2,1,0:T(8,128)(2,1)S(1)} %bitcast.14) | non-fusion elementwise | flops 589824 | bytes 3538944 | tf_op jit(solution)/shard_map/reshape | solution.py:416
  101.3 0.7 copy.19
  102.0 0.0 copy-done.8
  102.0 1.3 %copy.20 = bf16[128,64,128]{2,1,0:T(8,128)(2,1)} copy(bf16[128,64,128]{2,1,0:T(8,128)(2,1)S(1)} %copy-done.8) | data formatting | bytes 4194304
Async XLA Ops:
  1.4 1.3 %copy-start = (bf16[4,4,48,768]{3,2,1,0:T(8,128)(2,1)S(1)}, bf16[4,4,48,768]{3,2,1,0:T(8,128)(2,1)}, u32[]{:S(2)}) copy-start(bf16[4,4,48,768]{3,2,1,0:T(8,128)(2,1)} %param.16) | copy-start | bytes 3538948
  2.7 0.9 copy-start.1
  3.6 0.9 copy-start.2
  4.6 0.9 copy-start.3
  5.5 0.9 copy-start.4
  6.4 0.9 copy-start.5
  7.3 0.7 copy-start.6
  8.0 0.7 copy-start.7
  98.5 3.5 %copy-start.8 = (bf16[128,64,128]{2,1,0:T(8,128)(2,1)S(1)}, bf16[128,64,128]{2,1,0:T(8,128)(2,1)}, u32[]{:S(2)}) copy-start(bf16[128,64,128]{2,1,0:T(8,128)(2,1)} %get-tuple-element.20) | copy-start | bytes 6291460

commit v3 on v2

--- a/solution.py
+++ b/solution.py
@@ -196,6 +196,8 @@
         cot[1, h] = (contract(q_ref[h], full, 1, 1) * scale).astype(BF16)
         cot[2, h] = contract(cot[2, h], w_s[...], 1, 1).astype(BF16)
 
+    lag = 1
+
     def advance(h, s):
         ds_copy(h, s - 1).wait_recv()
         fold(ds if s == 1 else rs[s - 2], rs[s - 1], up_order, cb, s - 1, (h,))
@@ -209,14 +211,14 @@
         finish(h)
         for s in range(1, lc + 1):
 
-            @pl.when(h >= s)
+            @pl.when(h >= s + lag)
             def _():
-                advance(h - s, s)
+                advance(h - s - lag, s)
 
     def drain(now):
         for s in range(1, lc + 1):
-            if 0 <= now - s < heads:
-                advance(now - s, s)
+            if 0 <= now - s - lag < heads:
+                advance(now - s - lag, s)
 
     def dp_advance(c, s):
         dp_copy(c, s - 1).wait_recv()
@@ -244,7 +246,7 @@
     dt_copy(0).start()
     drain(heads + 1)
     dp_advance(0, 1)
-    for now in range(heads + 2, heads + lc):
+    for now in range(heads + 2, heads + lc + lag):
         drain(now)
 
     total = rs[lc - 1]
@@ -254,7 +256,34 @@
         sb_copy(step).start()
     rb[head] = sb[head]
 
-    for s in range(1, lc):
+    dt_advance(1)
+    dp_advance(1, 1)
+    dp_advance(0, 2)
+    for step in range(1, nh):
+        sb_copy(step).wait()
+    for peer in range(nh):
+        for h in range(heads):
+            xs[:, peer * heads + h, :] = rb[peer, h].astype(F32).T
+    columns = off_s[pl.ds(pl.multiple_of(copy * j, j), j), :]
+    bins = lax.broadcasted_iota(jnp.int32, (j, wide), 1).astype(F32)
+    reach = (BINS - 1) // 2
+    group = 8
+    channels = bw_ref.shape[0]
+
+    def pairs(g, acc):
+        for u in range(group):
+            i = g * group + u
+            x = xs[i].astype(BF16)
+            dpair_out[i] = contract(x, bw_ref[...], 0, 1).astype(BF16)
+            gap = columns - off_ref[head * tr + i].astype(F32)
+            hot = jnp.clip(gap, -reach, reach) + reach == bins
+            right = jnp.concatenate([pair_ref[i], hot.astype(F32).astype(BF16)], axis=1)
+            acc = acc + contract(x, right, 1, 0)
+        return acc
+
+    acc = jnp.zeros((nh * heads, channels + wide), F32)
+    acc = lax.fori_loop(0, tr // group // 2, pairs, acc)
+    for s in range(2, lc):
         if s <= lh:
             dt_advance(s)
         dp_advance(1, s)
@@ -265,6 +294,10 @@
     mine = tuple(cb[b] for b in reversed(range(lc)))
     pg[0][mine] = ps[0][lc - 1][...]
     pg_copy(0, lc - 1).start()
+    acc = lax.fori_loop(tr // group // 2, tr // group, pairs, acc)
+    first[copy] = acc
+    for step in range(1, n):
+        first_copy(step).start()
     dp_advance(1, lc)
     pg[1][mine] = ps[1][lc - 1][...]
     pg_copy(1, lc - 1).start()
@@ -275,37 +308,7 @@
             if s > 0:
                 pg_copy(c, s - 1).start()
 
-    for step in range(1, nh):
-        sb_copy(step).wait()
-    for peer in range(nh):
-        for h in range(heads):
-            xs[:, peer * heads + h, :] = rb[peer, h].astype(F32).T
-    columns = off_s[pl.ds(pl.multiple_of(copy * j, j), j), :]
-    bins = lax.broadcasted_iota(jnp.int32, (j, wide), 1).astype(F32)
-    reach = (BINS - 1) // 2
-    group = 8
-    channels = bw_ref.shape[0]
-
-    def pairs(g, acc):
-        for u in range(group):
-            i = g * group + u
-            x = xs[i].astype(BF16)
-            dpair_out[i] = contract(x, bw_ref[...], 0, 1).astype(BF16)
-            gap = columns - off_ref[head * tr + i].astype(F32)
-            hot = jnp.clip(gap, -reach, reach) + reach == bins
-            right = jnp.concatenate([pair_ref[i], hot.astype(F32).astype(BF16)], axis=1)
-            acc = acc + contract(x, right, 1, 0)
-        return acc
-
-    acc = jnp.zeros((nh * heads, channels + wide), F32)
-    acc = lax.fori_loop(0, tr // group // 2, pairs, acc)
     pg_advance(lc - 1)
-    acc = lax.fori_loop(tr // group // 2, tr // group, pairs, acc)
-    first[copy] = acc
-    for step in range(1, n):
-        first_copy(step).start()
-    for s in reversed(range(1, lc - 1)):
-        pg_advance(s)
     for step in range(1, n):
         first_copy(step).wait()
     acc = first[0]
@@ -314,7 +317,8 @@
     second[head] = acc
     for step in range(1, nh):
         second_copy(step).start()
-    pg_advance(0)
+    for s in reversed(range(lc - 1)):
+        pg_advance(s)
     for c in range(halves):
         dproj_out[:, c * dh : (c + 1) * dh] = pg[c][...].reshape(n * sr, dh)[:rows]
     for step in range(1, nh):
@@ -408,7 +412,7 @@
             dma((2, halves, lc)), dma((2, lh)), dma((2, nh)), dma((2, n)), dma((2, nh)),
         ],
         compiler_params=pltpu.CompilerParams(
-            collective_id=0, has_side_effects=True, vmem_limit_bytes=50 * 2**20
+            collective_id=0, has_side_effects=True, vmem_limit_bytes=62 * 2**20
         ),
     )(*args)
     return (

time: 104 us -> 104 us (level)
  local copies, waits for them, and re-layouts: 11.3 us -> 6.15 us
  Pallas kernels: 89.8 us -> 94.2 us
  other arithmetic: 1.65 us -> 2.92 us
    unnamed x21 -> x7, local copies, waits for them, and re-layouts: 10.1 us -> 3.41 us
    pallas_call x1, Pallas kernels: 89.8 us -> 94.2 us  [shards(): pl.pallas_call(functools.partial(main_kernel, n, nh, 1.0 / math.sqrt(hd))...]
    reshape x1, other arithmetic: 1.65 us -> 2.92 us  [shards(): d_proj.astype(F32).reshape(projections.shape)]
where the time goes in v3:
time: 104 us
  Pallas kernels  94.2 us (91%)
  local copies, waits for them, and re-layouts  6.15 us (6%)
  other arithmetic  2.92 us (3%)
    pallas_call x1, Pallas kernels, shards(): pl.pallas_call(functools.partial(main_kernel, n, nh, 1.0 / math.sqrt(hd))...  94.2 us
    unnamed x7, local copies, waits for them, and re-layouts  3.41 us
    reshape x1, other arithmetic, shards(): d_proj.astype(F32).reshape(projections.shape)  2.92 us

profile of v3, /device:TPU:0, one launch (start us, length us, event | category | flops | bytes accessed | tf_op | source)
XLA Modules:
  0.0 104.0 jit_solution(13866837161115674314)
XLA Ops:
  0.6 1.4 %copy.16.bw_ref = bf16[128,16]{1,0:T(8,128)(2,1)} copy(bf16[128,16]{0,1:T(8,128)(2,1)} %param.19) | data formatting | bytes 8192 | tf_op args[8]
  2.0 94.2 %shard_map.146 = (bf16[128,768]{1,0:T(8,128)(2,1)}, bf16[768,768]{1,0:T(8,128)(2,1)}, bf16[128,64,128]{2,1,0:T(8,128)(2,1)}, f32[16,256]{1,0:T(8,128)}) custom-call(s32[512]{0:T(512)} %off_ref.1, bf16[4,48,512]{2,1,0:T(8,128)(2,1)} %bitcast.15, bf16[4,48,512]{2,1,0:T(8,128)(2,1)} %bitcast.16, bf16[4,48,512]{2,1,0:T(8,128)(2,1)} %bitcast.17, ...), custom_call_target="tpu_custom_call" | custom-call | tf_op jit(solution)/shard_map/pallas_call | solution.py:371
  96.3 0.0 copy-start.1
  96.3 0.0 copy-start
  96.3 1.4 %slice.7 = f32[16,65]{1,0:T(8,128)} slice(f32[16,256]{1,0:T(8,128)} %get-tuple-element.12), slice={[0:16], [128:193]} | slice | bytes 8320 | tf_op jit(solution)/shard_map/slice | solution.py:423
  97.8 1.3 %slice_bitcast_fusion = f32[128,16]{0,1:T(8,128)} fusion(f32[16,256]{1,0:T(8,128)} %get-tuple-element.12), kind=kLoop, calls=%fused_computation | loop fusion | bytes 16384 | tf_op jit(solution)/shard_map/transpose | solution.py:422
  99.1 2.9 %convert.1 = f32[4,4,48,768]{3,2,1,0:T(8,128)} convert(bf16[4,4,48,768]{3,2,1,0:T(8,128)(2,1)} %bitcast.14) | non-fusion elementwise | flops 589824 | bytes 3538944 | tf_op jit(solution)/shard_map/reshape | solution.py:420
  102.0 0.0 copy-done.1
  102.0 0.7 copy.19
  102.7 0.0 copy-done
  102.7 1.3 %copy.20 = bf16[128,64,128]{2,1,0:T(8,128)(2,1)} copy(bf16[128,64,128]{2,1,0:T(8,128)(2,1)S(1)} %copy-done) | data formatting | bytes 4194304
Async XLA Ops:
  96.3 5.7 %copy-start.1 = (bf16[128,768]{1,0:T(8,128)(2,1)S(1)}, bf16[128,768]{1,0:T(8,128)(2,1)}, u32[]{:S(2)}) copy-start(bf16[128,768]{1,0:T(8,128)(2,1)} %get-tuple-element.9) | copy-start | bytes 589828
  96.3 6.4 %copy-start = (bf16[128,64,128]{2,1,0:T(8,128)(2,1)S(1)}, bf16[128,64,128]{2,1,0:T(8,128)(2,1)}, u32[]{:S(2)}) copy-start(bf16[128,64,128]{2,1,0:T(8,128)(2,1)} %get-tuple-element.20) | copy-start | bytes 6291460
